TPU v7x, 512 devices: a whole 4x4x16 slice. The times are simulated.
512 devices in a mesh: seq: 64 (over z, y), tensor: 4 (over x), group: 2 (over core).
Axes of the slice: x: 4, y: 4, z: 16, core: 2. Of those that a mesh axis runs over, the one named last changes fastest.
Arguments:
- queries: bfloat16 [32768, 4096], P('seq', ('tensor', 'group')), may hold values from -32 to 32
- cotangent: bfloat16 [32768, 4096], P('seq', ('tensor', 'group')), may hold values from -60 to 60
- encoded: bfloat16 [2, 192, 128, 4096], P(None, 'seq', None, ('tensor', 'group')), may hold values from -16 to 16
- neighbours: int32 [512, 2], P(('seq', 'tensor', 'group')), may hold values from 0 to 191, as said below
Outputs:
- query_grad: bfloat16 [32768, 4096], P('seq', ('tensor', 'group'))
- encoded_grad: bfloat16 [2, 192, 128, 4096], P(None, 'seq', None, ('tensor', 'group'))
Inputs may be any that keep to these rules, and one draw needn't show every extreme that they name: `neighbours`: the two ids of a row are different stretches with the same owner id // 3. The 8 rows of index s of seq name each owner o with o // 8 = s // 8 in exactly 1 row, and no other owner. Some stretches are named by many rows.
All inputs are finite; a program needn't handle non-finite values.
Results may differ from a plain program's by a relative error of at most 0.035.
Values may be sent and summed in bfloat16 or wider, within the bound.
A program may use at most 128 MiB of HBM per device.

v0:
```python
import math

import jax
import jax.numpy as jnp
from jax import lax
from jax.sharding import PartitionSpec as P

HD = 128


def for_sending(shard):

    def short(part):
        return part.astype(jnp.bfloat16) if part.dtype == jnp.float32 else part

    return jax.tree.map(short, shard)


def partner(block, axis, distance):
    count = lax.axis_size(axis)
    route = []
    for low in range(count):
        high = low | 1 << distance
        if high != low and high < count:
            route += [(low, high), (high, low)]
    return lax.ppermute(block, axis, route)


def from_behind(shard, axis, by):
    length = lax.axis_size(axis)
    pairs = [(i, i + by) for i in range(length) if 0 <= i + by < length]
    return lax.ppermute(shard, axis, pairs)


def slot_ranks(owners):
    length = owners.shape[-1]
    matches = owners[..., :, None] == owners[..., None, :]
    earlier = jnp.arange(length)[:, None] > jnp.arange(length)[None, :]
    return jnp.sum(jnp.logical_and(matches, earlier), axis=-1)


def split_pairs(member, half_width):
    return member.reshape((member.shape[0] // (2 * half_width), 2, half_width) + member.shape[1:])


def join_pairs(kept, moved):
    return jnp.stack([kept, moved], 1).reshape((-1,) + kept.shape[2:])


def request_path(query_slots, grad_slots, id_slots, group_size, capacity):
    for level in range(group_size.bit_length() - 1):
        half_width = (1 << level) * capacity
        query_split = split_pairs(query_slots, half_width)
        grad_split = split_pairs(grad_slots, half_width)
        id_split = split_pairs(id_slots, half_width)
        moved_query, moved_grad, moved_ids = partner(
            (query_split[:, 1], grad_split[:, 1], for_sending(id_split[:, 1])), "seq", level
        )
        query_slots = join_pairs(query_split[:, 0], moved_query)
        grad_slots = join_pairs(grad_split[:, 0], moved_grad)
        id_slots = join_pairs(id_split[:, 0], moved_ids)
    return (query_slots, grad_slots, id_slots)


def reply_path(answer_slots, group_size, capacity):
    for level in range(group_size.bit_length() - 1):
        half_width = (1 << level) * capacity
        answer_split = split_pairs(answer_slots, half_width)
        moved_answers = partner(answer_split[:, 1], "seq", level)
        answer_slots = join_pairs(answer_split[:, 0], moved_answers)
    return answer_slots


def owner_block(encoded, running, inputs, head_size):
    query_slots, grad_slots, id_slots = inputs
    slot_group, stretch_rows, feature_width = query_slots.shape
    head_count = feature_width // head_size
    stored = encoded.shape[1]
    neighbour_rows = encoded.shape[2]
    score_scale = 1.0 / math.sqrt(head_size)
    flat_ids = id_slots.reshape(-1)
    key_rows = encoded[0][flat_ids].reshape(slot_group, 2 * neighbour_rows, head_count, head_size)
    value_rows = encoded[1][flat_ids].reshape(slot_group, 2 * neighbour_rows, head_count, head_size)
    query_heads = query_slots.reshape(slot_group, stretch_rows, head_count, head_size)
    grad_heads = grad_slots.reshape(slot_group, stretch_rows, head_count, head_size)
    scores = (
        jnp.einsum("gqhd,gkhd->ghqk", query_heads, key_rows, preferred_element_type=jnp.float32)
        * score_scale
    )
    attention = jax.nn.softmax(scores, axis=-1)
    attention_low = attention.astype(jnp.bfloat16)
    grad_weights = jnp.einsum(
        "gqhd,gkhd->ghqk", grad_heads, value_rows, preferred_element_type=jnp.float32
    )
    row_delta = jnp.sum(attention_low.astype(jnp.float32) * grad_weights, axis=-1)
    grad_scores = attention * (grad_weights - row_delta[..., None])
    grad_scores_low = grad_scores.astype(jnp.bfloat16)
    query_part = jnp.einsum(
        "ghqk,gkhd->gqhd", grad_scores_low, key_rows, preferred_element_type=jnp.float32
    )
    query_part = (query_part * score_scale).astype(jnp.bfloat16)
    chosen = (id_slots[:, :, None] == jnp.arange(stored)[None, None, :]).astype(jnp.bfloat16)
    score_split = grad_scores_low.reshape(slot_group, head_count, stretch_rows, 2, neighbour_rows)
    weight_split = attention_low.reshape(slot_group, head_count, stretch_rows, 2, neighbour_rows)
    key_weights = jnp.einsum(
        "gjn,ghqjr->hnrgq", chosen, score_split, preferred_element_type=jnp.float32
    ).astype(jnp.bfloat16)
    value_weights = jnp.einsum(
        "gjn,ghqjr->hnrgq", chosen, weight_split, preferred_element_type=jnp.float32
    ).astype(jnp.bfloat16)
    key_update = (
        jnp.einsum("hnrgq,gqhd->nrhd", key_weights, query_heads, preferred_element_type=jnp.float32)
        * score_scale
    )
    value_update = jnp.einsum(
        "hnrgq,gqhd->nrhd", value_weights, grad_heads, preferred_element_type=jnp.float32
    )
    updates = jnp.stack(
        [
            key_update.reshape(stored, neighbour_rows, feature_width),
            value_update.reshape(stored, neighbour_rows, feature_width),
        ]
    )
    return (running + updates, query_part.reshape(slot_group, stretch_rows, feature_width))


def body(queries, cotangent, encoded, neighbours):
    head_size = HD
    feature_width = queries.shape[1]
    stored = encoded.shape[1]
    seq_count = lax.axis_size("seq")
    routes = lax.all_gather(neighbours, ("tensor", "group"), axis=0, tiled=True)
    stretch_count = routes.shape[0]
    group_size = min(seq_count, stretch_count)
    capacity = stretch_count // group_size
    stretch_rows = queries.shape[0] // stretch_count
    query_stretches = queries.reshape(stretch_count, stretch_rows, feature_width)
    grad_stretches = cotangent.reshape(stretch_count, stretch_rows, feature_width)
    next_query, next_grad = from_behind((query_stretches[0], grad_stretches[0]), "seq", -1)
    shifted_queries = jnp.concatenate([query_stretches[1:], next_query[None]], 0)
    shifted_grads = jnp.concatenate([grad_stretches[1:], next_grad[None]], 0)
    owners = routes[:, 0] // stored
    local_ids = routes - owners[:, None] * stored
    ranks = slot_ranks(owners)
    own_place = lax.axis_index("seq") % group_size
    slot_of = jnp.bitwise_xor(owners % group_size, own_place) * capacity + ranks
    send_query = (
        jnp.zeros((stretch_count, stretch_rows, feature_width), jnp.bfloat16)
        .at[slot_of]
        .set(shifted_queries)
    )
    send_grad = (
        jnp.zeros((stretch_count, stretch_rows, feature_width), jnp.bfloat16)
        .at[slot_of]
        .set(shifted_grads)
    )
    send_ids = jnp.zeros((stretch_count, 2), jnp.int32).at[slot_of].set(local_ids)
    arrived_query, arrived_grad, arrived_ids = request_path(
        send_query, send_grad, send_ids, group_size, capacity
    )
    slot_group = math.gcd(stretch_count, max(1, 512 // stretch_rows))
    block_count = stretch_count // slot_group

    def owner_step(running, inputs):
        return owner_block(encoded, running, inputs, head_size)

    initial = jnp.zeros((2, stored, encoded.shape[2], feature_width), jnp.float32)
    inputs = (
        arrived_query.reshape(block_count, slot_group, stretch_rows, feature_width),
        arrived_grad.reshape(block_count, slot_group, stretch_rows, feature_width),
        arrived_ids.reshape(block_count, slot_group, 2),
    )
    encoded_total, answers = lax.scan(owner_step, initial, inputs)
    answers = answers.reshape(stretch_count, stretch_rows, feature_width)
    returned = reply_path(answers, group_size, capacity)
    own_answers = returned[slot_of]
    leading = from_behind(own_answers[-1], "seq", 1)
    query_grad = jnp.concatenate([leading[None], own_answers[:-1]], 0).reshape(queries.shape)
    return (query_grad, encoded_total.astype(jnp.bfloat16))


def solution(mesh):
    placed = (
        P("seq", ("tensor", "group")),
        P("seq", ("tensor", "group")),
        P(None, "seq", None, ("tensor", "group")),
        P(("seq", "tensor", "group"), None),
    )
    return jax.shard_map(
        body,
        mesh=mesh,
        in_specs=placed,
        out_specs=(P("seq", ("tensor", "group")), P(None, "seq", None, ("tensor", "group"))),
        check_vma=False,
    )
```

profile of v0, /device:TPU:384, one launch (start us, length us, event | category | flops | bytes accessed | tf_op | source)
XLA Modules:
  0.0 126.9 jit_solution(5525281370836305777)
XLA Ops:
  0.7 10.8 %all-gather = s32[8,1,2]{2,1,0:T(1,128)S(1)} all-gather(s32[1,1,2]{2,1,0:T(1,128)} %bitcast.186), channel_id=1, replica_groups=mesh['seq'=64,'tensor'=4,'group'=2] {'tensor','group'}, dimensions={0}, use_global_device_ids=true | all-gather | bytes 72 | tf_op jit(solution)/shard_map/all_gather | solution.py:132
  11.7 0.2 convert_reduce_fusion
  11.9 0.6 scatter_custom_fusion
  12.5 0.1 copy.191
  12.6 3.5 %collective-permute-start = (s32[4,1,2]{0,2,1:T(2,128)S(1)}, s32[4,1,2]{0,2,1:T(2,128)S(1)}, u32[]{:S(2)}, u32[]{:S(2)}) collective-permute-start(s32[4,1,2]{0,2,1:T(2,128)S(1)} %bitcast.184), channel_id=1, source_target_pairs={{0,8},{8,0},{16,24},{24,16},{32,40},{40,32},{48,56},{56,48},{64,72... | collective-permute-start | bytes 104 | tf_op jit(solution)/shard_map/ppermute | solution.py:26
  16.1 0.8 slice.128
  16.9 5.7 %collective-permute-start.7 = (bf16[64,512]{1,0:T(8,128)(2,1)S(1)}, bf16[64,512]{1,0:T(8,128)(2,1)S(1)}, u32[]{:S(2)}, u32[]{:S(2)}) collective-permute-start(bf16[64,512]{1,0:T(8,128)(2,1)S(1)} %slice.128), channel_id=1, source_target_pairs={{8,0},{16,8},{24,16},{32,24},{40,32},{48,40},{56,48},{64,56},{72,6... | collective-permute-start | bytes 196616 | tf_op jit(solution)/shard_map/ppermute | solution.py:32
  22.7 0.8 slice.119
  23.5 3.2 %collective-permute-start.3 = (bf16[64,512]{1,0:T(8,128)(2,1)S(1)}, bf16[64,512]{1,0:T(8,128)(2,1)S(1)}, u32[]{:S(2)}, u32[]{:S(2)}) collective-permute-start(bf16[64,512]{1,0:T(8,128)(2,1)S(1)} %slice.119), channel_id=1, source_target_pairs={{8,0},{16,8},{24,16},{32,24},{40,32},{48,40},{56,48},{64,56},{72,6... | collective-permute-start | bytes 196616 | tf_op jit(solution)/shard_map/ppermute | solution.py:32
  26.7 0.1 copy.192
  27.1 0.1 copy.141
  27.2 1.9 %collective-permute-start.1 = (s32[2,2,2]{2,1,0:T(2,128)S(1)}, s32[2,2,2]{2,1,0:T(2,128)S(1)}, u32[]{:S(2)}, u32[]{:S(2)}) collective-permute-start(s32[2,2,2]{2,1,0:T(2,128)S(1)} %bitcast.182), channel_id=1, source_target_pairs={{0,16},{16,0},{8,24},{24,8},{32,48},{48,32},{40,56},{56,40},{64,80... | collective-permute-start | bytes 104 | tf_op jit(solution)/shard_map/ppermute | solution.py:26
  29.1 5.1 %collective-permute-done.1 = s32[2,2,2]{2,1,0:T(2,128)S(1)} collective-permute-done((s32[2,2,2]{2,1,0:T(2,128)S(1)}, s32[2,2,2]{2,1,0:T(2,128)S(1)}, u32[]{:S(2)}, u32[]{:S(2)}) %collective-permute-start.1) | collective-permute-done | bytes 64 | tf_op jit(solution)/shard_map/ppermute | solution.py:26
  34.2 0.1 copy.142
  34.3 0.1 copy.143
  34.7 0.8 scatter_fusion
  35.5 2.7 %collective-permute-start.4 = (bf16[4,1,64,512]{3,2,0,1:T(8,128)(2,1)S(1)}, bf16[4,1,64,512]{3,2,0,1:T(8,128)(2,1)S(1)}, u32[]{:S(2)}, u32[]{:S(2)}) collective-permute-start(bf16[4,1,64,512]{3,2,0,1:T(8,128)(2,1)S(1)} %get-tuple-element.51), channel_id=1, source_target_pairs={{0,8},{8,0},{16,24},{24,16},{32,40},{40,32},{48,56},{56,48},{64,72... | collective-permute-start | bytes 786440 | tf_op jit(solution)/shard_map/ppermute | solution.py:26
  38.3 0.8 scatter_fusion.1
  39.1 3.2 %collective-permute-start.8 = (bf16[4,1,64,512]{3,2,0,1:T(8,128)(2,1)S(1)}, bf16[4,1,64,512]{3,2,0,1:T(8,128)(2,1)S(1)}, u32[]{:S(2)}, u32[]{:S(2)}) collective-permute-start(bf16[4,1,64,512]{3,2,0,1:T(8,128)(2,1)S(1)} %get-tuple-element.57), channel_id=1, source_target_pairs={{0,8},{8,0},{16,24},{24,16},{32,40},{40,32},{48,56},{56,48},{64,72... | collective-permute-start | bytes 786440 | tf_op jit(solution)/shard_map/ppermute | solution.py:26
  42.3 3.9 %collective-permute-done.4 = bf16[4,1,64,512]{3,2,0,1:T(8,128)(2,1)S(1)} collective-permute-done((bf16[4,1,64,512]{3,2,0,1:T(8,128)(2,1)S(1)}, bf16[4,1,64,512]{3,2,0,1:T(8,128)(2,1)S(1)}, u32[]{:S(2)}, u32[]{:S(2)}) %collective-permute-start.4) | collective-permute-done | bytes 262176 | tf_op jit(solution)/shard_map/ppermute | solution.py:26
  46.3 1.9 %collective-permute-start.5 = (bf16[2,2,64,512]{3,2,0,1:T(8,128)(2,1)S(1)}, bf16[2,2,64,512]{3,2,0,1:T(8,128)(2,1)S(1)}, u32[]{:S(2)}, u32[]{:S(2)}) collective-permute-start(bf16[2,2,64,512]{3,2,0,1:T(8,128)(2,1)S(1)} %get-tuple-element.49), channel_id=1, source_target_pairs={{0,16},{16,0},{8,24},{24,8},{32,48},{48,32},{40,56},{56,40},{64,80... | collective-permute-start | bytes 786440 | tf_op jit(solution)/shard_map/ppermute | solution.py:26
  48.2 1.9 %collective-permute-start.2 = (s32[1,4,2]{1,2,0:T(2,128)S(1)}, s32[1,4,2]{1,2,0:T(2,128)S(1)}, u32[]{:S(2)}, u32[]{:S(2)}) collective-permute-start(s32[1,4,2]{1,2,0:T(2,128)S(1)} %get-tuple-element.63), channel_id=1, source_target_pairs={{0,32},{32,0},{8,40},{40,8},{16,48},{48,16},{24,56},{56,24},{64,96... | collective-permute-start | bytes 104 | tf_op jit(solution)/shard_map/ppermute | solution.py:26
  50.1 3.5 %collective-permute-done.2 = s32[1,4,2]{1,2,0:T(2,128)S(1)} collective-permute-done((s32[1,4,2]{1,2,0:T(2,128)S(1)}, s32[1,4,2]{1,2,0:T(2,128)S(1)}, u32[]{:S(2)}, u32[]{:S(2)}) %collective-permute-start.2) | collective-permute-done | bytes 64 | tf_op jit(solution)/shard_map/ppermute | solution.py:26
  53.7 0.1 copy.144
  53.8 0.1 reshape.151
  53.9 5.4 %collective-permute-start.9 = (bf16[2,2,64,512]{3,2,0,1:T(8,128)(2,1)S(1)}, bf16[2,2,64,512]{3,2,0,1:T(8,128)(2,1)S(1)}, u32[]{:S(2)}, u32[]{:S(2)}) collective-permute-start(bf16[2,2,64,512]{3,2,0,1:T(8,128)(2,1)S(1)} %get-tuple-element.55), channel_id=1, source_target_pairs={{0,16},{16,0},{8,24},{24,8},{32,48},{48,32},{40,56},{56,40},{64,80... | collective-permute-start | bytes 786440 | tf_op jit(solution)/shard_map/ppermute | solution.py:26
  59.4 0.7 slice_bitcast_fusion.9
  60.2 1.9 %collective-permute-start.6 = (bf16[1,4,64,512]{3,2,1,0:T(8,128)(2,1)}, bf16[1,4,64,512]{3,2,1,0:T(8,128)(2,1)}, u32[]{:S(2)}, u32[]{:S(2)}) collective-permute-start(bf16[1,4,64,512]{3,2,1,0:T(8,128)(2,1)} %get-tuple-element.47), channel_id=1, source_target_pairs={{0,32},{32,0},{8,40},{40,8},{16,48},{48,16},{24,56},{56,24},{64,96... | collective-permute-start | bytes 786440 | tf_op jit(solution)/shard_map/ppermute | solution.py:26
  62.1 1.6 %collective-permute-done.9 = bf16[2,2,64,512]{3,2,0,1:T(8,128)(2,1)S(1)} collective-permute-done((bf16[2,2,64,512]{3,2,0,1:T(8,128)(2,1)S(1)}, bf16[2,2,64,512]{3,2,0,1:T(8,128)(2,1)S(1)}, u32[]{:S(2)}, u32[]{:S(2)}) %collective-permute-start.9) | collective-permute-done | bytes 262176 | tf_op jit(solution)/shard_map/ppermute | solution.py:26
  63.8 0.7 slice_bitcast_fusion.6
  64.5 2.3 %collective-permute-start.10 = (bf16[1,4,64,512]{3,2,1,0:T(8,128)(2,1)}, bf16[1,4,64,512]{3,2,1,0:T(8,128)(2,1)}, u32[]{:S(2)}, u32[]{:S(2)}) collective-permute-start(bf16[1,4,64,512]{3,2,1,0:T(8,128)(2,1)} %get-tuple-element.53), channel_id=1, source_target_pairs={{0,32},{32,0},{8,40},{40,8},{16,48},{48,16},{24,56},{56,24},{64,96... | collective-permute-start | bytes 786440 | tf_op jit(solution)/shard_map/ppermute | solution.py:26
  66.8 0.7 gather_fusion
  67.5 2.0 %reshape.152 = bf16[8,256,4,128]{3,2,1,0:T(4,128)(2,1)} reshape(bf16[16,128,512]{2,1,0:T(8,128)(2,1)S(1)} %gather_fusion) | data formatting | bytes 4194304 | tf_op jit(solution)/shard_map/while/body/eval_jaxpr/reshape | solution.py:82
  69.6 0.7 gather_fusion.1
  70.3 2.1 %reshape.157 = bf16[8,256,4,128]{3,2,1,0:T(4,128)(2,1)} reshape(bf16[16,128,512]{2,1,0:T(8,128)(2,1)S(1)} %gather_fusion.1) | data formatting | bytes 4194304 | tf_op jit(solution)/shard_map/while/body/eval_jaxpr/reshape | solution.py:83
  72.3 1.1 pad_maximum_fusion.3
  73.5 0.9 reshape.154
  74.4 1.0 pad_maximum_fusion.6
  75.4 0.1 reshape.156
  75.6 3.6 %fusion.78 = (f32[8,4,64]{2,1,0:T(4,128)S(1)}, f32[8,4,64,256]{3,2,1,0:T(8,128)}) fusion(bf16[8,256,4,128]{3,2,1,0:T(4,128)(2,1)S(1)} %copy-done, bf16[8,64,4,128]{3,2,1,0:T(4,128)(2,1)} %reshape.154), kind=kOutput, calls=%fused_computation.122 | convolution fusion | flops 135790848 | bytes 4726784 | tf_op jit(solution)/shard_map/while/body/eval_jaxpr/sub | solution.py:90
  79.1 4.3 %multiply_reduce_fusion = (f32[8,4,64]{2,1,0:T(4,128)S(1)}, bf16[8,4,64,256]{3,2,1,0:T(8,128)(2,1)}, f32[8,4,64,256]{3,2,1,0:T(8,128)S(1)}) fusion(f32[8,4,64,256]{3,2,1,0:T(8,128)} %get-tuple-element.65, f32[8,4,64]{2,1,0:T(4,128)S(1)} %get-tuple-element.64, bf16[8,256,4,128]{3,2,1,0:T(4,128)(2,1)} %reshape.157, bf16[8,64,4,128]{3,2,1,0:T(4,128)(2,1)S(1)} %reshape.156), kind=kOutput, calls=%fused_computation.12 | convolution fusion | flops 136837120 | bytes 7880704 | tf_op jit(solution)/shard_map/while/body/eval_jaxpr/gqhd,gkhd->ghqk/dot_general | solution.py:92
  83.5 0.7 multiply_convert_fusion
  84.2 1.2 fusion.33
  85.4 0.3 reshape.160
  85.7 0.8 copy-done.7
  86.5 0.4 copy.156
  86.9 0.2 reshape_reshape.25
  87.1 2.6 %collective-permute-start.11 = (bf16[4,1,64,512]{3,2,0,1:T(8,128)(2,1)S(1)}, bf16[4,1,64,512]{3,2,0,1:T(8,128)(2,1)S(1)}, u32[]{:S(2)}, u32[]{:S(2)}) collective-permute-start(bf16[4,1,64,512]{3,2,0,1:T(8,128)(2,1)S(1)} %get-tuple-element.45), channel_id=1, source_target_pairs={{0,8},{8,0},{16,24},{24,16},{32,40},{40,32},{48,56},{56,48},{64,72... | collective-permute-start | bytes 786440 | tf_op jit(solution)/shard_map/ppermute | solution.py:26
  89.7 1.4 %convert_bitcast_fusion.1 = bf16[4,3,128,8,64]{2,1,4,0,3:T(4,128)(2,1)S(1)} fusion(bf16[8,4,64,2,128]{4,3,2,1,0:T(2,128)(2,1)S(1)} %reshape.160, s32[8,2]{1,0:T(8,128)S(1)} %bitcast.176), kind=kOutput, calls=%fused_computation.10 | convolution fusion | flops 3932208 | bytes 2621504 | tf_op jit(solution)/shard_map/while/body/eval_jaxpr/gjn,ghqjr->hnrgq/dot_general | solution.py:105
  91.1 0.5 fusion.39
  91.7 0.6 copy-done.2
  92.3 0.3 reshape.162
  92.6 3.3 %collective-permute-done.11 = bf16[4,1,64,512]{3,2,0,1:T(8,128)(2,1)S(1)} collective-permute-done((bf16[4,1,64,512]{3,2,0,1:T(8,128)(2,1)S(1)}, bf16[4,1,64,512]{3,2,0,1:T(8,128)(2,1)S(1)}, u32[]{:S(2)}, u32[]{:S(2)}) %collective-permute-start.11) | collective-permute-done | bytes 262176 | tf_op jit(solution)/shard_map/ppermute | solution.py:26
  95.9 7.3 %collective-permute-start.12 = (bf16[2,2,64,512]{3,2,0,1:T(8,128)(2,1)S(1)}, bf16[2,2,64,512]{3,2,0,1:T(8,128)(2,1)S(1)}, u32[]{:S(2)}, u32[]{:S(2)}) collective-permute-start(bf16[2,2,64,512]{3,2,0,1:T(8,128)(2,1)S(1)} %get-tuple-element.43), channel_id=1, source_target_pairs={{0,16},{16,0},{8,24},{24,8},{32,48},{48,32},{40,56},{56,40},{64,80... | collective-permute-start | bytes 786440 | tf_op jit(solution)/shard_map/ppermute | solution.py:26
  103.2 1.4 %convert_bitcast_fusion = bf16[4,3,128,8,64]{2,1,4,0,3:T(4,128)(2,1)S(1)} fusion(bf16[8,4,64,2,128]{4,3,2,1,0:T(2,128)(2,1)S(1)} %reshape.162, s32[8,2]{1,0:T(8,128)S(1)} %bitcast.177), kind=kOutput, calls=%fused_computation.9 | convolution fusion | flops 3932208 | bytes 2621504 | tf_op jit(solution)/shard_map/while/body/eval_jaxpr/gjn,ghqjr->hnrgq/dot_general | solution.py:108
  104.6 2.9 %collective-permute-done.12 = bf16[2,2,64,512]{3,2,0,1:T(8,128)(2,1)S(1)} collective-permute-done((bf16[2,2,64,512]{3,2,0,1:T(8,128)(2,1)S(1)}, bf16[2,2,64,512]{3,2,0,1:T(8,128)(2,1)S(1)}, u32[]{:S(2)}, u32[]{:S(2)}) %collective-permute-start.12) | collective-permute-done | bytes 262176 | tf_op jit(solution)/shard_map/ppermute | solution.py:26
  107.7 3.7 %collective-permute-start.13 = (bf16[1,4,64,512]{3,2,1,0:T(8,128)(2,1)S(1)}, bf16[1,4,64,512]{3,2,1,0:T(8,128)(2,1)S(1)}, u32[]{:S(2)}, u32[]{:S(2)}) collective-permute-start(bf16[1,4,64,512]{3,2,1,0:T(8,128)(2,1)S(1)} %get-tuple-element.41), channel_id=1, source_target_pairs={{0,32},{32,0},{8,40},{40,8},{16,48},{48,16},{24,56},{56,24},{64,96... | collective-permute-start | bytes 786440 | tf_op jit(solution)/shard_map/ppermute | solution.py:26
  111.4 0.5 fusion.36
  112.0 3.9 %collective-permute-done.13 = bf16[1,4,64,512]{3,2,1,0:T(8,128)(2,1)S(1)} collective-permute-done((bf16[1,4,64,512]{3,2,1,0:T(8,128)(2,1)S(1)}, bf16[1,4,64,512]{3,2,1,0:T(8,128)(2,1)S(1)}, u32[]{:S(2)}, u32[]{:S(2)}) %collective-permute-start.13) | collective-permute-done | bytes 262176 | tf_op jit(solution)/shard_map/ppermute | solution.py:26
  116.0 0.6 gather_fusion.2
  116.6 1.9 %collective-permute-start.14 = (bf16[64,512]{1,0:T(8,128)(2,1)S(1)}, bf16[64,512]{1,0:T(8,128)(2,1)S(1)}, u32[]{:S(2)}, u32[]{:S(2)}) collective-permute-start(bf16[64,512]{1,0:T(8,128)(2,1)S(1)} %slice_bitcast_fusion.11), channel_id=1, source_target_pairs={{0,8},{8,16},{16,24},{24,32},{32,40},{40,48},{48,56},{56,64},{64,7... | collective-permute-start | bytes 196616 | tf_op jit(solution)/shard_map/ppermute | solution.py:32
  118.6 1.2 copy.167
  119.8 6.3 %collective-permute-done.14 = bf16[64,512]{1,0:T(8,128)(2,1)S(1)} collective-permute-done((bf16[64,512]{1,0:T(8,128)(2,1)S(1)}, bf16[64,512]{1,0:T(8,128)(2,1)S(1)}, u32[]{:S(2)}, u32[]{:S(2)}) %collective-permute-start.14) | collective-permute-done | bytes 65568 | tf_op jit(solution)/shard_map/ppermute | solution.py:32
  126.1 0.8 pad_maximum_fusion.9
  (64 shorter events, 1.5 us)
Async XLA Ops:
  0.6 33.9 %slice-start.1 = ((bf16[512,512]{1,0:T(8,128)(2,1)}), bf16[448,512]{1,0:T(8,128)(2,1)S(1)}, s32[]{:S(2)}) async-start(bf16[512,512]{1,0:T(8,128)(2,1)} %param.4), calls=%async_computation.1 | async-start | bytes 917504 | tf_op jit(solution)/shard_map/slice | solution.py:140
  0.6 26.2 %copy-start.3 = (bf16[2,3,128,512]{3,2,1,0:T(8,128)(2,1)S(1)}, bf16[2,3,128,512]{3,2,1,0:T(8,128)(2,1)}, u32[]{:S(2)}) copy-start(bf16[2,3,128,512]{3,2,1,0:T(8,128)(2,1)} %param.6) | copy-start | bytes 2359300
  12.6 14.3 %collective-permute-start = (s32[4,1,2]{0,2,1:T(2,128)S(1)}, s32[4,1,2]{0,2,1:T(2,128)S(1)}, u32[]{:S(2)}, u32[]{:S(2)}) collective-permute-start(s32[4,1,2]{0,2,1:T(2,128)S(1)} %bitcast.184), channel_id=1, source_target_pairs={{0,8},{8,0},{16,24},{24,16},{32,40},{40,32},{48,56},{56,48},{64,72... | collective-permute-start | bytes 104 | tf_op jit(solution)/shard_map/ppermute | solution.py:26
  16.9 21.2 %collective-permute-start.7 = (bf16[64,512]{1,0:T(8,128)(2,1)S(1)}, bf16[64,512]{1,0:T(8,128)(2,1)S(1)}, u32[]{:S(2)}, u32[]{:S(2)}) collective-permute-start(bf16[64,512]{1,0:T(8,128)(2,1)S(1)} %slice.128), channel_id=1, source_target_pairs={{8,0},{16,8},{24,16},{32,24},{40,32},{48,40},{56,48},{64,56},{72,6... | collective-permute-start | bytes 196616 | tf_op jit(solution)/shard_map/ppermute | solution.py:32
  23.5 11.0 %collective-permute-start.3 = (bf16[64,512]{1,0:T(8,128)(2,1)S(1)}, bf16[64,512]{1,0:T(8,128)(2,1)S(1)}, u32[]{:S(2)}, u32[]{:S(2)}) collective-permute-start(bf16[64,512]{1,0:T(8,128)(2,1)S(1)} %slice.119), channel_id=1, source_target_pairs={{8,0},{16,8},{24,16},{32,24},{40,32},{48,40},{56,48},{64,56},{72,6... | collective-permute-start | bytes 196616 | tf_op jit(solution)/shard_map/ppermute | solution.py:32
  27.2 7.0 %collective-permute-start.1 = (s32[2,2,2]{2,1,0:T(2,128)S(1)}, s32[2,2,2]{2,1,0:T(2,128)S(1)}, u32[]{:S(2)}, u32[]{:S(2)}) collective-permute-start(s32[2,2,2]{2,1,0:T(2,128)S(1)} %bitcast.182), channel_id=1, source_target_pairs={{0,16},{16,0},{8,24},{24,8},{32,48},{48,32},{40,56},{56,40},{64,80... | collective-permute-start | bytes 104 | tf_op jit(solution)/shard_map/ppermute | solution.py:26
  34.5 3.6 %slice-start = ((bf16[512,512]{1,0:T(8,128)(2,1)}), bf16[448,512]{1,0:T(8,128)(2,1)S(1)}, s32[]{:S(2)}) async-start(bf16[512,512]{1,0:T(8,128)(2,1)} %param.5), calls=%async_computation | async-start | bytes 917504 | tf_op jit(solution)/shard_map/slice | solution.py:141
  35.5 10.7 %collective-permute-start.4 = (bf16[4,1,64,512]{3,2,0,1:T(8,128)(2,1)S(1)}, bf16[4,1,64,512]{3,2,0,1:T(8,128)(2,1)S(1)}, u32[]{:S(2)}, u32[]{:S(2)}) collective-permute-start(bf16[4,1,64,512]{3,2,0,1:T(8,128)(2,1)S(1)} %get-tuple-element.51), channel_id=1, source_target_pairs={{0,8},{8,0},{16,24},{24,16},{32,40},{40,32},{48,56},{56,48},{64,72... | collective-permute-start | bytes 786440 | tf_op jit(solution)/shard_map/ppermute | solution.py:26
  39.1 14.8 %collective-permute-start.8 = (bf16[4,1,64,512]{3,2,0,1:T(8,128)(2,1)S(1)}, bf16[4,1,64,512]{3,2,0,1:T(8,128)(2,1)S(1)}, u32[]{:S(2)}, u32[]{:S(2)}) collective-permute-start(bf16[4,1,64,512]{3,2,0,1:T(8,128)(2,1)S(1)} %get-tuple-element.57), channel_id=1, source_target_pairs={{0,8},{8,0},{16,24},{24,16},{32,40},{40,32},{48,56},{56,48},{64,72... | collective-permute-start | bytes 786440 | tf_op jit(solution)/shard_map/ppermute | solution.py:26
  46.3 13.1 %collective-permute-start.5 = (bf16[2,2,64,512]{3,2,0,1:T(8,128)(2,1)S(1)}, bf16[2,2,64,512]{3,2,0,1:T(8,128)(2,1)S(1)}, u32[]{:S(2)}, u32[]{:S(2)}) collective-permute-start(bf16[2,2,64,512]{3,2,0,1:T(8,128)(2,1)S(1)} %get-tuple-element.49), channel_id=1, source_target_pairs={{0,16},{16,0},{8,24},{24,8},{32,48},{48,32},{40,56},{56,40},{64,80... | collective-permute-start | bytes 786440 | tf_op jit(solution)/shard_map/ppermute | solution.py:26
  48.2 5.5 %collective-permute-start.2 = (s32[1,4,2]{1,2,0:T(2,128)S(1)}, s32[1,4,2]{1,2,0:T(2,128)S(1)}, u32[]{:S(2)}, u32[]{:S(2)}) collective-permute-start(s32[1,4,2]{1,2,0:T(2,128)S(1)} %get-tuple-element.63), channel_id=1, source_target_pairs={{0,32},{32,0},{8,40},{40,8},{16,48},{48,16},{24,56},{56,24},{64,96... | collective-permute-start | bytes 104 | tf_op jit(solution)/shard_map/ppermute | solution.py:26
  53.9 9.8 %collective-permute-start.9 = (bf16[2,2,64,512]{3,2,0,1:T(8,128)(2,1)S(1)}, bf16[2,2,64,512]{3,2,0,1:T(8,128)(2,1)S(1)}, u32[]{:S(2)}, u32[]{:S(2)}) collective-permute-start(bf16[2,2,64,512]{3,2,0,1:T(8,128)(2,1)S(1)} %get-tuple-element.55), channel_id=1, source_target_pairs={{0,16},{16,0},{8,24},{24,8},{32,48},{48,32},{40,56},{56,40},{64,80... | collective-permute-start | bytes 786440 | tf_op jit(solution)/shard_map/ppermute | solution.py:26
  60.2 12.2 %collective-permute-start.6 = (bf16[1,4,64,512]{3,2,1,0:T(8,128)(2,1)}, bf16[1,4,64,512]{3,2,1,0:T(8,128)(2,1)}, u32[]{:S(2)}, u32[]{:S(2)}) collective-permute-start(bf16[1,4,64,512]{3,2,1,0:T(8,128)(2,1)} %get-tuple-element.47), channel_id=1, source_target_pairs={{0,32},{32,0},{8,40},{40,8},{16,48},{48,16},{24,56},{56,24},{64,96... | collective-permute-start | bytes 786440 | tf_op jit(solution)/shard_map/ppermute | solution.py:26
  64.5 9.9 %collective-permute-start.10 = (bf16[1,4,64,512]{3,2,1,0:T(8,128)(2,1)}, bf16[1,4,64,512]{3,2,1,0:T(8,128)(2,1)}, u32[]{:S(2)}, u32[]{:S(2)}) collective-permute-start(bf16[1,4,64,512]{3,2,1,0:T(8,128)(2,1)} %get-tuple-element.53), channel_id=1, source_target_pairs={{0,32},{32,0},{8,40},{40,8},{16,48},{48,16},{24,56},{56,24},{64,96... | collective-permute-start | bytes 786440 | tf_op jit(solution)/shard_map/ppermute | solution.py:26
  72.3 3.2 %copy-start = (bf16[8,256,4,128]{3,2,1,0:T(4,128)(2,1)S(1)}, bf16[8,256,4,128]{3,2,1,0:T(4,128)(2,1)}, u32[]{:S(2)}) copy-start(bf16[8,256,4,128]{3,2,1,0:T(4,128)(2,1)} %reshape.152) | copy-start | bytes 6291460
  75.6 3.6 %copy-start.4 = (bf16[8,64,4,128]{3,2,1,0:T(4,128)(2,1)}, bf16[8,64,4,128]{3,2,1,0:T(4,128)(2,1)S(1)}, u32[]{:S(2)}) copy-start(bf16[8,64,4,128]{3,2,1,0:T(4,128)(2,1)S(1)} %reshape.156) | copy-start | bytes 1572868
  79.1 4.3 %copy-start.1 = (f32[8,4,64,256]{3,2,1,0:T(8,128)S(1)}, f32[8,4,64,256]{3,2,1,0:T(8,128)}, u32[]{:S(2)}) copy-start(f32[8,4,64,256]{3,2,1,0:T(8,128)} %get-tuple-element.65) | copy-start | bytes 6291460
  85.4 1.0 copy-start.7
  87.1 8.7 %collective-permute-start.11 = (bf16[4,1,64,512]{3,2,0,1:T(8,128)(2,1)S(1)}, bf16[4,1,64,512]{3,2,0,1:T(8,128)(2,1)S(1)}, u32[]{:S(2)}, u32[]{:S(2)}) collective-permute-start(bf16[4,1,64,512]{3,2,0,1:T(8,128)(2,1)S(1)} %get-tuple-element.45), channel_id=1, source_target_pairs={{0,8},{8,0},{16,24},{24,16},{32,40},{40,32},{48,56},{56,48},{64,72... | collective-permute-start | bytes 786440 | tf_op jit(solution)/shard_map/ppermute | solution.py:26
  89.7 1.4 %copy-start.6 = (bf16[8,64,4,128]{3,2,1,0:T(4,128)(2,1)S(1)}, bf16[8,64,4,128]{3,2,1,0:T(4,128)(2,1)}, u32[]{:S(2)}) copy-start(bf16[8,64,4,128]{3,2,1,0:T(4,128)(2,1)} %reshape.154) | copy-start | bytes 1572868
  91.1 1.2 copy-start.2
  95.9 11.6 %collective-permute-start.12 = (bf16[2,2,64,512]{3,2,0,1:T(8,128)(2,1)S(1)}, bf16[2,2,64,512]{3,2,0,1:T(8,128)(2,1)S(1)}, u32[]{:S(2)}, u32[]{:S(2)}) collective-permute-start(bf16[2,2,64,512]{3,2,0,1:T(8,128)(2,1)S(1)} %get-tuple-element.43), channel_id=1, source_target_pairs={{0,16},{16,0},{8,24},{24,8},{32,48},{48,32},{40,56},{56,40},{64,80... | collective-permute-start | bytes 786440 | tf_op jit(solution)/shard_map/ppermute | solution.py:26
  104.6 6.8 %copy-start.5 = (bf16[8,64,4,128]{3,2,1,0:T(4,128)(2,1)S(1)}, bf16[8,64,4,128]{3,2,1,0:T(4,128)(2,1)}, u32[]{:S(2)}) copy-start(bf16[8,64,4,128]{3,2,1,0:T(4,128)(2,1)} %copy-done.4) | copy-start | bytes 1572868
  107.7 8.3 %collective-permute-start.13 = (bf16[1,4,64,512]{3,2,1,0:T(8,128)(2,1)S(1)}, bf16[1,4,64,512]{3,2,1,0:T(8,128)(2,1)S(1)}, u32[]{:S(2)}, u32[]{:S(2)}) collective-permute-start(bf16[1,4,64,512]{3,2,1,0:T(8,128)(2,1)S(1)} %get-tuple-element.41), channel_id=1, source_target_pairs={{0,32},{32,0},{8,40},{40,8},{16,48},{48,16},{24,56},{56,24},{64,96... | collective-permute-start | bytes 786440 | tf_op jit(solution)/shard_map/ppermute | solution.py:26
  116.6 9.5 %collective-permute-start.14 = (bf16[64,512]{1,0:T(8,128)(2,1)S(1)}, bf16[64,512]{1,0:T(8,128)(2,1)S(1)}, u32[]{:S(2)}, u32[]{:S(2)}) collective-permute-start(bf16[64,512]{1,0:T(8,128)(2,1)S(1)} %slice_bitcast_fusion.11), channel_id=1, source_target_pairs={{0,8},{8,16},{16,24},{24,32},{32,40},{40,48},{48,56},{56,64},{64,7... | collective-permute-start | bytes 196616 | tf_op jit(solution)/shard_map/ppermute | solution.py:32
where the time goes:
time: 128 us; the launch traced here: 127 us
  starting transfers between devices  49.2 us (38%)
  waiting for transfers between devices  30.6 us (24%)
  local copies, waits for them, and re-layouts  17.7 us (14%)
  matrix products  12.9 us (10%)
  blocking collectives  10.8 us (8%)
  other arithmetic  4.54 us (4%)
    ppermute x12, starting transfers between devices, partner(): return lax.ppermute(block, axis, route)  38.3 us
    ppermute x12, waiting for transfers between devices, partner(): return lax.ppermute(block, axis, route)  24.3 us
    ppermute x3, starting transfers between devices, from_behind(): return lax.ppermute(shard, axis, pairs)  10.8 us
    all_gather x1, blocking collectives, body(): routes = lax.all_gather(neighbours, ('tensor', 'group'), axis=0, tiled=True)  10.8 us
    ppermute x3, waiting for transfers between devices, from_behind(): return lax.ppermute(shard, axis, pairs)  6.26 us
    dot_general x1, matrix products, owner_block(): jnp.einsum('gqhd,gkhd->ghqk', grad_heads, value_rows, preferred_element_t...  4.34 us
    unnamed x22, local copies, waits for them, and re-layouts  4.2 us
    sub x1, matrix products, owner_block(): attention = jax.nn.softmax(scores, axis=-1)  3.55 us
  transfers between devices with their start and end apart: 15, of which 8 were waited for; matrix products, arithmetic and copies ran while one was open for 15% of the time, Pallas kernels for 0%

commit v1 on v0

v1 whole, which is shorter than its diff:
```python
import functools
import math

import jax
import jax.numpy as jnp
from jax import lax
from jax.experimental import pallas as pl
from jax.experimental.pallas import tpu as pltpu
from jax.sharding import PartitionSpec as P

HD = 128
GROUP = 8
MESH = pl.DeviceIdType.MESH


def kernel(heads, rows, stored, keys, q_ref, g_ref, e_ref, n_ref, oq_ref, oe_ref, *scratch):
    x = scratch[:heads]
    send = scratch[heads:2 * heads]
    recv = scratch[2 * heads:3 * heads]
    rsend = scratch[3 * heads:4 * heads]
    rrecv = scratch[4 * heads:5 * heads]
    out = scratch[5 * heads:6 * heads]
    (first, enc, egrad, ids, codes, fsem, xsem, esem, isem, osem, gsem, id_send, id_recv, sh_send, sh_recv,
     rq_send, rq_recv, rp_send, rp_recv, bk_send, bk_recv) = scratch[6 * heads:]
    s = lax.axis_index("seq")
    t = lax.axis_index("tensor")
    c = lax.axis_index("group")
    count = lax.axis_size("seq")
    tensors = lax.axis_size("tensor")
    groups = lax.axis_size("group")
    members = tensors * groups
    place = lax.rem(s, GROUP)
    base = s - place
    member = t * groups + c
    has_before, has_after = s > 0, s < count - 1

    def owner_device(k):
        return (base + jnp.bitwise_xor(place, k), t, c)

    def member_device(d):
        other = jnp.bitwise_xor(member, d)
        return (s, other // groups, lax.rem(other, groups))

    barrier = pltpu.get_barrier_semaphore()
    for device in (
        [owner_device(k) for k in range(1, GROUP)]
        + [member_device(d) for d in range(1, members)]
    ):
        pl.semaphore_signal(barrier, inc=1, device_id=device, device_id_type=MESH)

    @pl.when(has_before)
    def _():
        pl.semaphore_signal(barrier, inc=1, device_id=(s - 1, t, c), device_id_type=MESH)

    @pl.when(has_after)
    def _():
        pl.semaphore_signal(barrier, inc=1, device_id=(s + 1, t, c), device_id_type=MESH)

    def columns(h):
        return pl.ds(h * HD, HD)

    id_load = pltpu.make_async_copy(n_ref, ids, isem)
    id_load.start()
    first_loads, x_loads = [], []
    for h in range(heads):
        first_loads.append([
            pltpu.make_async_copy(q_ref.at[0, :, columns(h)], first.at[h, pl.ds(0, rows)], fsem.at[h, 0]),
            pltpu.make_async_copy(g_ref.at[0, :, columns(h)], first.at[h, pl.ds(rows, rows)], fsem.at[h, 1]),
        ])
        for load in first_loads[h]:
            load.start()
    for h in range(heads):
        x_loads.append([
            pltpu.make_async_copy(
                q_ref.at[pl.ds(1, GROUP - 1), :, columns(h)], x[h].at[pl.ds(0, GROUP - 1), pl.ds(0, rows)], xsem.at[h, 0]),
            pltpu.make_async_copy(
                g_ref.at[pl.ds(1, GROUP - 1), :, columns(h)], x[h].at[pl.ds(0, GROUP - 1), pl.ds(rows, rows)], xsem.at[h, 1]),
        ])
        for load in x_loads[h]:
            load.start()
    enc_load = pltpu.make_async_copy(e_ref, enc, esem)
    enc_load.start()

    id_load.wait()
    near, far = ids[0, 0], ids[0, 1]
    owner = near // stored
    excluded = (3 - (near - owner * stored)) - (far - owner * stored)
    codes[member, 0] = lax.rem(owner, GROUP) * 4 + excluded

    with jax.named_scope("barrier"):
        pl.semaphore_wait(barrier, GROUP - 1 + members - 1 + has_before.astype(jnp.int32) + has_after.astype(jnp.int32))

    id_copies = []
    for d in range(1, members):
        copy = pltpu.make_async_remote_copy(
            codes.at[member], codes.at[member], id_send.at[d], id_recv.at[d], device_id=member_device(d), device_id_type=MESH)
        copy.start()
        id_copies.append(copy)
    shifts = []
    for h in range(heads):
        for load in first_loads[h]:
            load.wait()

        copy = pltpu.make_async_remote_copy(
            first.at[h], x[h].at[GROUP - 1], sh_send.at[h], sh_recv.at[h], device_id=(s - 1, t, c), device_id_type=MESH)
        pl.when(has_before)(copy.start)
        shifts.append(copy)

    with jax.named_scope("ids"):
        for copy in id_copies:
            copy.wait_recv()
    code = [codes[j, 0] for j in range(GROUP)]
    slot_of = [jnp.bitwise_xor(code[j] // 4, place) for j in range(GROUP)]
    row_of, left_out = [], []
    for k in range(GROUP):
        row, gone = jnp.int32(0), jnp.int32(0)
        for j in range(GROUP):
            here = slot_of[j] == k
            row = jnp.where(here, jnp.int32(j), row)
            gone = jnp.where(here, lax.rem(code[j], 4), gone)
        row_of.append(row)
        left_out.append(gone)

    both = 2 * rows
    requests = []
    for h in range(heads):
        for load in x_loads[h]:
            load.wait()
        with jax.named_scope("shift"):
            pl.when(has_after)(shifts[h].wait_recv)

        @pl.when(jnp.logical_not(has_after))
        def _():
            x[h][GROUP - 1] = jnp.zeros(x[h].shape[1:], x[h].dtype)

        requests.append([])
        for k in range(GROUP):
            target = recv[h] if k == 0 else send[h]
            target[k, pl.ds(0, both)] = x[h][row_of[k]]
            if h == 0:
                target[k, pl.ds(both, 16)] = jnp.full((16, HD), left_out[k].astype(jnp.float32), jnp.float32).astype(jnp.bfloat16)
            if k:
                copy = pltpu.make_async_remote_copy(
                    send[h].at[k], recv[h].at[k], rq_send.at[h, k], rq_recv.at[h, k],
                    device_id=owner_device(k), device_id_type=MESH)
                copy.start()
                requests[h].append(copy)

    enc_load.wait()
    scale = 1.0 / math.sqrt(HD)
    contract_minor = (((1,), (1,)), ((), ()))
    contract_major = (((0,), (0,)), ((), ()))
    replies, egrad_stores = [], []
    bias = None
    for h in range(heads):
        with jax.named_scope("requests"):
            for copy in requests[h]:
                copy.wait_recv()
        if h == 0:
            lane = lax.broadcasted_iota(jnp.int32, (16, HD), 1)
            parts = []
            for k in range(0, GROUP, 2):
                low = recv[0][k, pl.ds(both, 16)].astype(jnp.float32)
                high = recv[0][k + 1, pl.ds(both, 16)].astype(jnp.float32)
                parts.append(jnp.where(lane < rows, low, high)[0:1])
            gone = jnp.concatenate(parts, axis=1)
            bias = [jnp.where(gone == float(n), jnp.float32(-1e30), jnp.float32(0.0)) for n in range(stored)]
        queries = recv[h][:, pl.ds(0, rows)].reshape(GROUP * rows, HD)
        grads = recv[h][:, pl.ds(rows, rows)].reshape(GROUP * rows, HD)
        key_rows = enc[0, :, :, h * HD:(h + 1) * HD].reshape(stored * keys, HD)
        value_rows = enc[1, :, :, h * HD:(h + 1) * HD].reshape(stored * keys, HD)
        scores = lax.dot_general(key_rows, queries, contract_minor, preferred_element_type=jnp.float32)
        scores = jnp.concatenate([scores[n * keys:(n + 1) * keys] * scale + bias[n] for n in range(stored)], axis=0)
        scores = jnp.exp(scores - jnp.max(scores, axis=0, keepdims=True))
        probs = scores * (1.0 / jnp.sum(scores, axis=0, keepdims=True))
        probs_low = probs.astype(jnp.bfloat16)
        grad_probs = lax.dot_general(value_rows, grads, contract_minor, preferred_element_type=jnp.float32)
        delta = jnp.sum(probs_low.astype(jnp.float32) * grad_probs, axis=0, keepdims=True)
        grad_scores = (probs * (grad_probs - delta)).astype(jnp.bfloat16)
        answer = (lax.dot_general(grad_scores, key_rows, contract_major, preferred_element_type=jnp.float32) * scale)
        answer = answer.astype(jnp.bfloat16).reshape(GROUP, rows, HD)
        rrecv[h][0] = answer[0]
        rsend[h][...] = answer[1:]
        replies.append([])
        for k in range(1, GROUP):
            copy = pltpu.make_async_remote_copy(
                rsend[h].at[k - 1], rrecv[h].at[k], rp_send.at[h, k], rp_recv.at[h, k],
                device_id=owner_device(k), device_id_type=MESH)
            copy.start()
            replies[h].append(copy)
        key_part = lax.dot_general(grad_scores, queries, (((1,), (0,)), ((), ())), preferred_element_type=jnp.float32) * scale
        value_part = lax.dot_general(probs_low, grads, (((1,), (0,)), ((), ())), preferred_element_type=jnp.float32)
        egrad[h, 0] = key_part.astype(jnp.bfloat16).reshape(stored, keys, HD)
        egrad[h, 1] = value_part.astype(jnp.bfloat16).reshape(stored, keys, HD)
        store = pltpu.make_async_copy(egrad.at[h], oe_ref.at[:, :, :, columns(h)], gsem.at[h])
        store.start()
        egrad_stores.append(store)

    backs, out_stores = [], []
    for h in range(heads):
        with jax.named_scope("replies"):
            for copy in replies[h]:
                copy.wait_recv()
        out[h][GROUP - 1] = rrecv[h][slot_of[GROUP - 1]]
        copy = pltpu.make_async_remote_copy(
            out[h].at[GROUP - 1], oq_ref.at[0, :, columns(h)], bk_send.at[h], bk_recv.at[h],
            device_id=(s + 1, t, c), device_id_type=MESH)
        pl.when(has_after)(copy.start)
        backs.append(copy)
        for j in range(GROUP - 1):
            out[h][j] = rrecv[h][slot_of[j]]
        store = pltpu.make_async_copy(
            out[h].at[pl.ds(0, GROUP - 1)], oq_ref.at[pl.ds(1, GROUP - 1), :, columns(h)], osem.at[h])
        store.start()
        out_stores.append(store)

    with jax.named_scope("sends"):
        for copy in id_copies:
            copy.wait_send()
        for h in range(heads):
            pl.when(has_before)(shifts[h].wait_send)
            for copy in requests[h] + replies[h]:
                copy.wait_send()
            egrad_stores[h].wait()

    @pl.when(s == 0)
    def _():
        for h in range(heads):
            first[h] = jnp.zeros(first.shape[1:], first.dtype)
            zero = pltpu.make_async_copy(first.at[h, pl.ds(0, rows)], oq_ref.at[0, :, columns(h)], fsem.at[h, 0])
            zero.start()
            zero.wait()

    with jax.named_scope("stores"):
        for h in range(heads):
            out_stores[h].wait()
            pl.when(has_after)(backs[h].wait_send)
    with jax.named_scope("backs"):
        for h in range(heads):
            pl.when(has_before)(backs[h].wait_recv)


def body(queries, cotangent, encoded, neighbours):
    width = queries.shape[1]
    heads = width // HD
    rows = queries.shape[0] // GROUP
    stored, keys = encoded.shape[1], encoded.shape[2]
    members = lax.axis_size("tensor") * lax.axis_size("group")
    bf16 = jnp.bfloat16
    both = 2 * rows
    dma = pltpu.SemaphoreType.DMA
    scratch = (
        [pltpu.VMEM((GROUP, both, HD), bf16) for _ in range(heads)]
        + [pltpu.VMEM((GROUP, both + (16 if h == 0 else 0), HD), bf16) for h in range(heads)]
        + [pltpu.VMEM((GROUP, both + (16 if h == 0 else 0), HD), bf16) for h in range(heads)]
        + [pltpu.VMEM((GROUP - 1, rows, HD), bf16) for _ in range(heads)]
        + [pltpu.VMEM((GROUP, rows, HD), bf16) for _ in range(heads)]
        + [pltpu.VMEM((GROUP, rows, HD), bf16) for _ in range(heads)]
        + [
            pltpu.VMEM((heads, both, HD), bf16),
            pltpu.VMEM(encoded.shape, bf16),
            pltpu.VMEM((heads, 2, stored, keys, HD), bf16),
            pltpu.SMEM((1, 2), jnp.int32),
            pltpu.SMEM((GROUP, 128), jnp.int32),
            dma((heads, 2)), dma((heads, 2)), dma, dma, dma((heads,)), dma((heads,)),
            dma((members,)), dma((members,)), dma((heads,)), dma((heads,)),
            dma((heads, GROUP)), dma((heads, GROUP)), dma((heads, GROUP)), dma((heads, GROUP)),
            dma((heads,)), dma((heads,)),
        ]
    )
    hbm = pl.BlockSpec(memory_space=pltpu.HBM)
    anywhere = pl.BlockSpec(memory_space=pl.ANY)
    query_grad, encoded_grad = pl.pallas_call(
        functools.partial(kernel, heads, rows, stored, keys),
        out_shape=(
            jax.ShapeDtypeStruct((GROUP, rows, width), bf16),
            jax.ShapeDtypeStruct(encoded.shape, bf16),
        ),
        in_specs=[hbm] * 4,
        out_specs=(anywhere, anywhere),
        scratch_shapes=scratch,
        compiler_params=pltpu.CompilerParams(
            collective_id=0, has_side_effects=True, vmem_limit_bytes=48 * 2**20
        ),
        cost_estimate=pl.CostEstimate(flops=10**9, bytes_accessed=3 * 2**20, transcendentals=10**6),
        name="retrieval_grads",
    )(*[
        pltpu.with_memory_space_constraint(operand, pltpu.HBM)
        for operand in (queries.reshape(GROUP, rows, width), cotangent.reshape(GROUP, rows, width), encoded, neighbours)
    ])
    return query_grad.reshape(queries.shape), encoded_grad


def solution(mesh):
    placed = (
        P("seq", ("tensor", "group")),
        P("seq", ("tensor", "group")),
        P(None, "seq", None, ("tensor", "group")),
        P(("seq", "tensor", "group"), None),
    )
    return jax.shard_map(
        body,
        mesh=mesh,
        in_specs=placed,
        out_specs=(P("seq", ("tensor", "group")), P(None, "seq", None, ("tensor", "group"))),
        check_vma=False,
    )
```

time: 128 us -> 40.7 us (0.32)
  the two profiles are of different devices: /device:TPU:384 before, /device:TPU:102 now
where the time goes in v1:
time: 40.7 us; the launch traced here: 40.6 us
  Pallas kernels  38.2 us (94%)
  local copies, waits for them, and re-layouts  1.67 us (4%)
  between operations  0.64 us (2%)
    pallas_call x1, Pallas kernels, body(): pl.pallas_call(functools.partial(kernel, heads, rows, stored, keys), out_...  38.2 us
    unnamed x2, local copies, waits for them, and re-layouts  1.67 us

profile of v1, /device:TPU:102, one launch (start us, length us, event | category | flops | bytes accessed | tf_op | source)
XLA Modules:
  0.0 40.6 jit_solution(7949062100979644388)
XLA Ops:
  0.6 38.2 %retrieval_grads.1 = (bf16[8,64,512]{2,1,0:T(8,128)(2,1)S(1)}, bf16[2,3,128,512]{3,2,1,0:T(8,128)(2,1)S(1)}) custom-call(bf16[8,64,512]{2,1,0:T(8,128)(2,1)} %bitcast.4, bf16[8,64,512]{2,1,0:T(8,128)(2,1)} %bitcast.5, bf16[2,3,128,512]{3,2,1,0:T(8,128)(2,1)} %e_ref.1, s32[1,2]{1,0:T(1,128)} %n_ref.1), custom_call_target="tpu_custom_call" | custom-call | flops 1000000000 | bytes 3145728 | tf_op jit(solution)/shard_map/retrieval_grads/pallas_call | solution.py:273
  38.9 0.8 %copy.8 = bf16[512,512]{1,0:T(8,128)(2,1)} copy(bf16[512,512]{1,0:T(8,128)(2,1)S(1)} %bitcast.3) | data formatting | bytes 1048576
  39.7 0.9 %copy.9 = bf16[2,3,128,512]{3,2,1,0:T(8,128)(2,1)} copy(bf16[2,3,128,512]{3,2,1,0:T(8,128)(2,1)S(1)} %get-tuple-element.9) | data formatting | bytes 1572864

commit v2 on v1

v2 whole, which is shorter than its diff:
```python
import functools
import math

import jax
import jax.numpy as jnp
from jax import lax
from jax.experimental import pallas as pl
from jax.experimental.pallas import tpu as pltpu
from jax.sharding import PartitionSpec as P

HD = 128
GROUP = 8
SLOTS = (7, 6, 5, 4, 3, 2, 1)
MESH = pl.DeviceIdType.MESH


def kernel(heads, rows, stored, keys, q_ref, g_ref, e_ref, n_ref, oq_ref, oe_ref, *scratch):
    x = scratch[:heads]
    rrecv = scratch[heads:2 * heads]
    out = scratch[2 * heads:3 * heads]
    (send, recv, rsend, first, enc, egrad, low_probs, low_grads, turned, tiles, gone_tiles, bias, ids, codes, fsem, xsem, esem,
     isem, osem, gsem, id_send, id_recv, tl_send, tl_recv, sh_send, sh_recv, rq_send, rq_recv, rp_send, rp_recv, bk_send,
     bk_recv, ready) = scratch[3 * heads:]
    both = 2 * rows
    width = 2 * rows
    pairs = GROUP // 2
    s = lax.axis_index("seq")
    t = lax.axis_index("tensor")
    c = lax.axis_index("group")
    count = lax.axis_size("seq")
    tensors = lax.axis_size("tensor")
    groups = lax.axis_size("group")
    members = tensors * groups
    place = lax.rem(s, GROUP)
    base = s - place
    member = t * groups + c
    has_before, has_after = s > 0, s < count - 1

    def owner_device(k):
        return (base + jnp.bitwise_xor(place, k), t, c)

    def member_device(d):
        other = jnp.bitwise_xor(member, d)
        return (s, other // groups, lax.rem(other, groups))

    barrier = pltpu.get_barrier_semaphore()
    for d in range(1, members):
        pl.semaphore_signal(barrier, inc=1, device_id=member_device(d), device_id_type=MESH)

    @pl.when(jnp.logical_and(has_before, place != 1))
    def _():
        pl.semaphore_signal(barrier, inc=1, device_id=(s - 1, t, c), device_id_type=MESH)

    @pl.when(has_after)
    def _():
        pl.semaphore_signal(barrier, inc=1, device_id=(s + 1, t, c), device_id_type=MESH)

    for k in SLOTS:

        @pl.when(place != k)
        def _():
            pl.semaphore_signal(barrier, inc=1, device_id=owner_device(k), device_id_type=MESH)

    def columns(h):
        return pl.ds(h * HD, HD)

    id_load = pltpu.make_async_copy(n_ref, ids, isem)
    id_load.start()
    first_loads, x_loads, enc_loads = [], [], []
    for h in range(heads):
        first_loads.append([
            pltpu.make_async_copy(ref.at[0, :, columns(h)], first.at[h, pl.ds(half * rows, rows)], fsem.at[h, half])
            for half, ref in enumerate((q_ref, g_ref))
        ])
        for load in first_loads[h]:
            load.start()
    for h in range(heads):
        enc_loads.append(pltpu.make_async_copy(e_ref.at[:, :, :, columns(h)], enc.at[h], esem.at[h]))
        enc_loads[h].start()
    for h in range(heads):
        x_loads.append([
            pltpu.make_async_copy(
                ref.at[pl.ds(1, GROUP - 1), :, columns(h)],
                x[h].at[pl.ds(0, GROUP - 1), pl.ds(half * rows, rows)], xsem.at[h, half])
            for half, ref in enumerate((q_ref, g_ref))
        ])
        for load in x_loads[h]:
            load.start()

    id_load.wait()
    near, far = ids[0, 0], ids[0, 1]
    owner = near // stored
    excluded = (3 - (near - owner * stored)) - (far - owner * stored)
    codes[member, 0] = lax.rem(owner, GROUP) * 4 + excluded

    mates = jnp.where(place == 0, 0, GROUP - 1 + has_after.astype(jnp.int32))
    pl.semaphore_wait(barrier, members - 1 + has_before.astype(jnp.int32) + mates)

    @pl.when(place != 0)
    def _():
        pl.semaphore_signal(ready, inc=1, device_id=(base, t, c), device_id_type=MESH)

    id_copies = []
    for d in range(1, members):
        copy = pltpu.make_async_remote_copy(
            codes.at[member], codes.at[member], id_send.at[d], id_recv.at[d], device_id=member_device(d), device_id_type=MESH)
        copy.start()
        id_copies.append(copy)
    shifts = []
    for h in range(heads):
        for load in first_loads[h]:
            load.wait()
        copy = pltpu.make_async_remote_copy(
            first.at[h], x[h].at[GROUP - 1], sh_send.at[h], sh_recv.at[h], device_id=(s - 1, t, c), device_id_type=MESH)
        pl.when(has_before)(copy.start)
        shifts.append(copy)

    for load in enc_loads:
        load.wait()

    @pl.loop(0, heads)
    def _(h):
        turned[h] = enc[h, 0].reshape(stored * keys, HD).T

    for copy in id_copies:
        copy.wait_recv()
    code = [codes[j, 0] for j in range(GROUP)]
    slot_of = [jnp.bitwise_xor(code[j] // 4, place) for j in range(GROUP)]
    row_of, left_out = [], []
    for k in range(GROUP):
        row, gone = jnp.int32(0), jnp.int32(0)
        for j in range(GROUP):
            here = slot_of[j] == k
            row = jnp.where(here, jnp.int32(j), row)
            gone = jnp.where(here, lax.rem(code[j], 4), gone)
        row_of.append(row)
        left_out.append(gone)

    def tile_copy(k):
        return pltpu.make_async_remote_copy(
            tiles.at[k], gone_tiles.at[k], tl_send.at[k], tl_recv.at[k], device_id=owner_device(k), device_id_type=MESH)

    def request(h, k):
        return pltpu.make_async_remote_copy(
            send.at[h, k], recv.at[h, k], rq_send.at[h, k], rq_recv.at[h, k], device_id=owner_device(k), device_id_type=MESH)

    def reply(h, k, target):
        return pltpu.make_async_remote_copy(
            rsend.at[h, k], target.at[k], rp_send.at[h, k], rp_recv.at[h, k], device_id=owner_device(k), device_id_type=MESH)

    def egrad_store(h):
        start = h * HD if isinstance(h, int) else pl.multiple_of(h * HD, HD)
        return pltpu.make_async_copy(egrad.at[h], oe_ref.at[:, :, :, pl.ds(start, HD)], gsem.at[h])

    @pl.when(place == 0)
    def _():
        pl.semaphore_wait(ready, GROUP - 1)

    for k in SLOTS:
        tiles[k] = jnp.full(tiles.shape[1:], left_out[k].astype(jnp.float32), jnp.float32)
        tile_copy(k).start()
    gone_tiles[0] = jnp.full(tiles.shape[1:], left_out[0].astype(jnp.float32), jnp.float32)
    for h in range(heads):
        for load in x_loads[h]:
            load.wait()
        pl.when(has_after)(shifts[h].wait_recv)

        @pl.when(jnp.logical_not(has_after))
        def _():
            x[h][GROUP - 1] = jnp.zeros(x[h].shape[1:], x[h].dtype)

        for k in SLOTS:
            send[h, k] = x[h][row_of[k]]
            request(h, k).start()
        recv[h, 0] = x[h][row_of[0]]

    scale = 1.0 / math.sqrt(HD)
    minor = (((1,), (1,)), ((), ()))
    plain = (((1,), (0,)), ((), ()))
    lane = lax.broadcasted_iota(jnp.int32, tiles.shape[1:], 1)
    for k in SLOTS:
        tile_copy(k).wait_recv()
    for p in range(pairs):
        gone = jnp.where(lane < rows, gone_tiles[2 * p], gone_tiles[2 * p + 1])
        for m in range(stored):
            bias[p, m] = jnp.where(gone == float(m), jnp.float32(-1e30), jnp.float32(0.0))

    blocks = 2
    span = GROUP // blocks

    @pl.loop(0, heads * blocks)
    def _(step):
        h = step // blocks if blocks > 1 else step
        p = blocks - 1 - lax.rem(step, blocks) if blocks > 1 else 0
        k = span * p
        for i in range(span - 1, -1, -1):
            if i:
                request(h, k + i).wait_recv()
            elif blocks > 1:

                @pl.when(k > 0)
                def _():
                    request(h, k).wait_recv()

        queries = recv[h, pl.ds(k, span), pl.ds(0, rows)].reshape(span * rows, HD)
        grads = recv[h, pl.ds(k, span), pl.ds(rows, rows)].reshape(span * rows, HD)
        key_rows = enc[h, 0].reshape(stored * keys, HD)
        value_rows = enc[h, 1].reshape(stored * keys, HD)
        scores = lax.dot_general(key_rows, queries, minor, preferred_element_type=jnp.float32)
        grad_probs = lax.dot_general(value_rows, grads, minor, preferred_element_type=jnp.float32)
        masks = [jnp.concatenate([bias[p * (span // 2) + i, m][0:1] for i in range(span // 2)], axis=1) for m in range(stored)]
        scores = jnp.concatenate([scores[m * keys:(m + 1) * keys] * scale + masks[m] for m in range(stored)], axis=0)
        scores = jnp.exp(scores - jnp.max(scores, axis=0, keepdims=True))
        probs = scores * (1.0 / jnp.sum(scores, axis=0, keepdims=True))
        probs_low = probs.astype(jnp.bfloat16)
        delta = jnp.sum(probs_low.astype(jnp.float32) * grad_probs, axis=0, keepdims=True)
        grad_scores = (probs * (grad_probs - delta)).astype(jnp.bfloat16)
        low_probs[p] = probs_low
        low_grads[p] = grad_scores
        answer = lax.dot_general(turned[h], grad_scores, plain, preferred_element_type=jnp.float32) * scale
        rsend[h, pl.ds(k, span)] = answer.T.astype(jnp.bfloat16).reshape(span, rows, HD)
        for g in range(heads):

            @pl.when(h == g)
            def _():
                for i in range(span - 1, 0, -1):
                    reply(g, k + i, rrecv[g]).start()

                @pl.when(k > 0)
                def _():
                    reply(g, k, rrecv[g]).start()

                @pl.when(k == 0)
                def _():
                    rrecv[g][0] = rsend[g, 0]

        @pl.when(jnp.int32(k) == 0)
        def _():
            queries = recv[h, :, pl.ds(0, rows)].reshape(GROUP * rows, HD)
            grads = recv[h, :, pl.ds(rows, rows)].reshape(GROUP * rows, HD)
            score_parts = jnp.concatenate([low_grads[i] for i in range(blocks)], axis=1)
            prob_parts = jnp.concatenate([low_probs[i] for i in range(blocks)], axis=1)
            key_part = lax.dot_general(score_parts, queries, plain, preferred_element_type=jnp.float32) * scale
            value_part = lax.dot_general(prob_parts, grads, plain, preferred_element_type=jnp.float32)
            egrad[h, 0] = key_part.astype(jnp.bfloat16).reshape(stored, keys, HD)
            egrad[h, 1] = value_part.astype(jnp.bfloat16).reshape(stored, keys, HD)
            egrad_store(h).start()

    backs, out_stores = [], []
    for h in range(heads):
        for k in SLOTS:
            reply(h, k, rrecv[h]).wait_recv()
        out[h][GROUP - 1] = rrecv[h][slot_of[GROUP - 1]]
        copy = pltpu.make_async_remote_copy(
            out[h].at[GROUP - 1], oq_ref.at[0, :, columns(h)], bk_send.at[h], bk_recv.at[h],
            device_id=(s + 1, t, c), device_id_type=MESH)
        pl.when(has_after)(copy.start)
        backs.append(copy)
        for j in range(GROUP - 1):
            out[h][j] = rrecv[h][slot_of[j]]
        store = pltpu.make_async_copy(
            out[h].at[pl.ds(0, GROUP - 1)], oq_ref.at[pl.ds(1, GROUP - 1), :, columns(h)], osem.at[h])
        store.start()
        out_stores.append(store)

    for copy in id_copies:
        copy.wait_send()
    for k in SLOTS:
        tile_copy(k).wait_send()
    for h in range(heads):
        pl.when(has_before)(shifts[h].wait_send)
        for k in SLOTS:
            request(h, k).wait_send()
            reply(h, k, rrecv[h]).wait_send()
        egrad_store(h).wait()

    @pl.when(jnp.logical_not(has_before))
    def _():
        for h in range(heads):
            first[h] = jnp.zeros(first.shape[1:], first.dtype)
            zero = pltpu.make_async_copy(first.at[h, pl.ds(0, rows)], oq_ref.at[0, :, columns(h)], fsem.at[h, 0])
            zero.start()
            zero.wait()

    for h in range(heads):
        out_stores[h].wait()
        pl.when(has_after)(backs[h].wait_send)
    for h in range(heads):
        pl.when(has_before)(backs[h].wait_recv)


def finish(q_in, e_in, q_out, e_out, sems):
    copies = []
    for i, (source, target) in enumerate(((q_in, q_out), (e_in.at[0], e_out.at[0]), (e_in.at[1], e_out.at[1]))):
        copy = pltpu.make_async_copy(source, target, sems.at[i])
        copy.start()
        copies.append(copy)
    for copy in copies:
        copy.wait()


def body(queries, cotangent, encoded, neighbours):
    width = queries.shape[1]
    heads = width // HD
    rows = queries.shape[0] // GROUP
    stored, keys = encoded.shape[1], encoded.shape[2]
    members = lax.axis_size("tensor") * lax.axis_size("group")
    bf16 = jnp.bfloat16
    both = 2 * rows
    dma = pltpu.SemaphoreType.DMA
    scratch = (
        [pltpu.VMEM((GROUP, both, HD), bf16) for _ in range(heads)]
        + [pltpu.VMEM((GROUP, rows, HD), bf16) for _ in range(2 * heads)]
        + [
            pltpu.VMEM((heads, GROUP, both, HD), bf16),
            pltpu.VMEM((heads, GROUP, both, HD), bf16),
            pltpu.VMEM((heads, GROUP, rows, HD), bf16),
            pltpu.VMEM((heads, both, HD), bf16),
            pltpu.VMEM((heads, 2, stored, keys, HD), bf16),
            pltpu.VMEM((heads, 2, stored, keys, HD), bf16),
            pltpu.VMEM((2, stored * keys, GROUP // 2 * rows), bf16),
            pltpu.VMEM((2, stored * keys, GROUP // 2 * rows), bf16),
            pltpu.VMEM((heads, HD, stored * keys), bf16),
            pltpu.VMEM((GROUP, 8, HD), jnp.float32),
            pltpu.VMEM((GROUP, 8, HD), jnp.float32),
            pltpu.VMEM((GROUP // 2, stored, 8, HD), jnp.float32),
            pltpu.SMEM((1, 2), jnp.int32),
            pltpu.SMEM((GROUP, 128), jnp.int32),
            dma((heads, 2)), dma((heads, 2)), dma((heads,)), dma, dma((heads,)), dma((heads,)),
            dma((members,)), dma((members,)), dma((GROUP,)), dma((GROUP,)), dma((heads,)), dma((heads,)),
            dma((heads, GROUP)), dma((heads, GROUP)), dma((heads, GROUP)), dma((heads, GROUP)),
            dma((heads,)), dma((heads,)), pltpu.SemaphoreType.REGULAR,
        ]
    )
    hbm = pl.BlockSpec(memory_space=pltpu.HBM)
    anywhere = pl.BlockSpec(memory_space=pl.ANY)
    query_grad, encoded_grad = pl.pallas_call(
        functools.partial(kernel, heads, rows, stored, keys),
        out_shape=(
            jax.ShapeDtypeStruct((GROUP, rows, width), bf16),
            jax.ShapeDtypeStruct(encoded.shape, bf16),
        ),
        in_specs=[hbm] * 4,
        out_specs=(anywhere, anywhere),
        scratch_shapes=scratch,
        compiler_params=pltpu.CompilerParams(
            collective_id=0, has_side_effects=True, vmem_limit_bytes=48 * 2**20
        ),
        cost_estimate=pl.CostEstimate(flops=10**9, bytes_accessed=3 * 2**20, transcendentals=10**6),
        name="retrieval_grads",
    )(*[
        pltpu.with_memory_space_constraint(operand, pltpu.HBM)
        for operand in (queries.reshape(GROUP, rows, width), cotangent.reshape(GROUP, rows, width), encoded, neighbours)
    ])
    query_grad, encoded_grad = pl.pallas_call(
        finish,
        out_shape=(
            pltpu.HBM((GROUP, rows, width), bf16),
            pltpu.HBM(encoded.shape, bf16),
        ),
        in_specs=[anywhere] * 2,
        out_specs=(anywhere, anywhere),
        scratch_shapes=[dma((3,))],
        compiler_params=pltpu.CompilerParams(vmem_limit_bytes=2**20),
        cost_estimate=pl.CostEstimate(flops=0, bytes_accessed=3 * 2**20, transcendentals=0),
        name="retrieval_finish",
    )(query_grad, encoded_grad)
    return query_grad.reshape(queries.shape), encoded_grad


def solution(mesh):
    placed = (
        P("seq", ("tensor", "group")),
        P("seq", ("tensor", "group")),
        P(None, "seq", None, ("tensor", "group")),
        P(("seq", "tensor", "group"), None),
    )
    return jax.shard_map(
        body,
        mesh=mesh,
        in_specs=placed,
        out_specs=(P("seq", ("tensor", "group")), P(None, "seq", None, ("tensor", "group"))),
        check_vma=False,
    )
```

time: 40.7 us -> 37.8 us (0.929)
  the two profiles are of different devices: /device:TPU:102 before, /device:TPU:384 now
where the time goes in v2:
time: 37.8 us; the launch traced here: 37.7 us
  Pallas kernels  37.1 us (98%)
  between operations  0.64 us (2%)
    pallas_call x1, Pallas kernels, body(): pl.pallas_call(functools.partial(kernel, heads, rows, stored, keys), out_...  36 us
    pallas_call x1, Pallas kernels, body(): pl.pallas_call(finish, out_shape=(pltpu.HBM((GROUP, rows, width), bf16),...  1.08 us

profile of v2, /device:TPU:384, one launch (start us, length us, event | category | flops | bytes accessed | tf_op | source)
XLA Modules:
  0.0 37.7 jit_solution(6984507383615088244)
XLA Ops:
  0.6 36.0 %retrieval_grads.1 = (bf16[8,64,512]{2,1,0:T(8,128)(2,1)S(1)}, bf16[2,3,128,512]{3,2,1,0:T(8,128)(2,1)S(1)}) custom-call(bf16[8,64,512]{2,1,0:T(8,128)(2,1)} %bitcast.3, bf16[8,64,512]{2,1,0:T(8,128)(2,1)} %bitcast.4, bf16[2,3,128,512]{3,2,1,0:T(8,128)(2,1)} %e_ref.1, s32[1,2]{1,0:T(1,128)} %n_ref.1), custom_call_target="tpu_custom_call" | custom-call | flops 1000000000 | bytes 3145728 | tf_op jit(solution)/shard_map/retrieval_grads/pallas_call | solution.py:337
  36.6 1.1 %retrieval_finish.1 = (bf16[8,64,512]{2,1,0:T(8,128)(2,1)}, bf16[2,3,128,512]{3,2,1,0:T(8,128)(2,1)}) custom-call(bf16[8,64,512]{2,1,0:T(8,128)(2,1)S(1)} %get-tuple-element.6.q_in, bf16[2,3,128,512]{3,2,1,0:T(8,128)(2,1)S(1)} %get-tuple-element.7.e_in), custom_call_target="tpu_custom_call" | custom-call | bytes 3145728 | tf_op jit(solution)/shard_map/retrieval_finish/pallas_call | solution.py:355

commit v3 on v2

--- a/solution.py
+++ b/solution.py
@@ -10,7 +10,7 @@
 
 HD = 128
 GROUP = 8
-SLOTS = (7, 6, 5, 4, 3, 2, 1)
+SLOTS = (6, 7, 5, 4, 2, 3, 1)
 MESH = pl.DeviceIdType.MESH
 
 
@@ -246,8 +246,20 @@
             egrad[h, 1] = value_part.astype(jnp.bfloat16).reshape(stored, keys, HD)
             egrad_store(h).start()
 
+    for copy in id_copies:
+        copy.wait_send()
+    for k in SLOTS:
+        tile_copy(k).wait_send()
+    for h in range(heads):
+        pl.when(has_before)(shifts[h].wait_send)
+        for k in SLOTS:
+            request(h, k).wait_send()
     backs, out_stores = [], []
     for h in range(heads):
+        if h:
+            egrad_store(h - 1).wait()
+            for k in SLOTS:
+                reply(h - 1, k, rrecv[h - 1]).wait_send()
         for k in SLOTS:
             reply(h, k, rrecv[h]).wait_recv()
         out[h][GROUP - 1] = rrecv[h][slot_of[GROUP - 1]]
@@ -263,16 +275,8 @@
         store.start()
         out_stores.append(store)
 
-    for copy in id_copies:
-        copy.wait_send()
-    for k in SLOTS:
-        tile_copy(k).wait_send()
-    for h in range(heads):
-        pl.when(has_before)(shifts[h].wait_send)
-        for k in SLOTS:
-            request(h, k).wait_send()
-            reply(h, k, rrecv[h]).wait_send()
-        egrad_store(h).wait()
+    for k in SLOTS:
+        reply(heads - 1, k, rrecv[heads - 1]).wait_send()
 
     @pl.when(jnp.logical_not(has_before))
     def _():
@@ -282,6 +286,7 @@
             zero.start()
             zero.wait()
 
+    egrad_store(heads - 1).wait()
     for h in range(heads):
         out_stores[h].wait()
         pl.when(has_after)(backs[h].wait_send)

time: 37.8 us -> 37.7 us (level)
  no operation moved by 1% of the time
where the time goes in v3:
time: 37.7 us; the launch traced here: 37.6 us
  Pallas kernels  36.9 us (98%)
  between operations  0.64 us (2%)
    pallas_call x1, Pallas kernels, body(): pl.pallas_call(functools.partial(kernel, heads, rows, stored, keys), out_...  35.8 us
    pallas_call x1, Pallas kernels, body(): pl.pallas_call(finish, out_shape=(pltpu.HBM((GROUP, rows, width), bf16),...  1.08 us

profile of v3, /device:TPU:384, one launch (start us, length us, event | category | flops | bytes accessed | tf_op | source)
XLA Modules:
  0.0 37.6 jit_solution(14301595741031580721)
XLA Ops:
  0.6 35.8 %retrieval_grads.1 = (bf16[8,64,512]{2,1,0:T(8,128)(2,1)S(1)}, bf16[2,3,128,512]{3,2,1,0:T(8,128)(2,1)S(1)}) custom-call(bf16[8,64,512]{2,1,0:T(8,128)(2,1)} %bitcast.3, bf16[8,64,512]{2,1,0:T(8,128)(2,1)} %bitcast.4, bf16[2,3,128,512]{3,2,1,0:T(8,128)(2,1)} %e_ref.1, s32[1,2]{1,0:T(1,128)} %n_ref.1), custom_call_target="tpu_custom_call" | custom-call | flops 1000000000 | bytes 3145728 | tf_op jit(solution)/shard_map/retrieval_grads/pallas_call | solution.py:342
  36.5 1.1 %retrieval_finish.1 = (bf16[8,64,512]{2,1,0:T(8,128)(2,1)}, bf16[2,3,128,512]{3,2,1,0:T(8,128)(2,1)}) custom-call(bf16[8,64,512]{2,1,0:T(8,128)(2,1)S(1)} %get-tuple-element.6.q_in, bf16[2,3,128,512]{3,2,1,0:T(8,128)(2,1)S(1)} %get-tuple-element.7.e_in), custom_call_target="tpu_custom_call" | custom-call | bytes 3145728 | tf_op jit(solution)/shard_map/retrieval_finish/pallas_call | solution.py:360

commit v4 on v3

--- a/solution.py
+++ b/solution.py
@@ -11,6 +11,7 @@
 HD = 128
 GROUP = 8
 SLOTS = (6, 7, 5, 4, 2, 3, 1)
+OTHERS = (2, 1, 3, 4, 6, 5, 7)
 MESH = pl.DeviceIdType.MESH
 
 
@@ -169,8 +170,9 @@
         def _():
             x[h][GROUP - 1] = jnp.zeros(x[h].shape[1:], x[h].dtype)
 
-        for k in SLOTS:
-            send[h, k] = x[h][row_of[k]]
+        for low, high in zip(SLOTS, OTHERS):
+            k = jnp.where(c == 0, jnp.int32(low), jnp.int32(high))
+            send[h, k] = x[h][jnp.where(c == 0, row_of[low], row_of[high])]
             request(h, k).start()
         recv[h, 0] = x[h][row_of[0]]
 

time: 37.7 us -> 37.7 us (level)
  no operation moved by 1% of the time
where the time goes in v4:
time: 37.7 us; the launch traced here: 37.6 us
  Pallas kernels  36.9 us (98%)
  between operations  0.64 us (2%)
    pallas_call x1, Pallas kernels, body(): pl.pallas_call(functools.partial(kernel, heads, rows, stored, keys), out_...  35.8 us
    pallas_call x1, Pallas kernels, body(): pl.pallas_call(finish, out_shape=(pltpu.HBM((GROUP, rows, width), bf16),...  1.08 us

profile of v4, /device:TPU:384, one launch (start us, length us, event | category | flops | bytes accessed | tf_op | source)
XLA Modules:
  0.0 37.6 jit_solution(1290319041248056796)
XLA Ops:
  0.6 35.8 %retrieval_grads.1 = (bf16[8,64,512]{2,1,0:T(8,128)(2,1)S(1)}, bf16[2,3,128,512]{3,2,1,0:T(8,128)(2,1)S(1)}) custom-call(bf16[8,64,512]{2,1,0:T(8,128)(2,1)} %bitcast.3, bf16[8,64,512]{2,1,0:T(8,128)(2,1)} %bitcast.4, bf16[2,3,128,512]{3,2,1,0:T(8,128)(2,1)} %e_ref.1, s32[1,2]{1,0:T(1,128)} %n_ref.1), custom_call_target="tpu_custom_call" | custom-call | flops 1000000000 | bytes 3145728 | tf_op jit(solution)/shard_map/retrieval_grads/pallas_call | solution.py:344
  36.5 1.1 %retrieval_finish.1 = (bf16[8,64,512]{2,1,0:T(8,128)(2,1)}, bf16[2,3,128,512]{3,2,1,0:T(8,128)(2,1)}) custom-call(bf16[8,64,512]{2,1,0:T(8,128)(2,1)S(1)} %get-tuple-element.6.q_in, bf16[2,3,128,512]{3,2,1,0:T(8,128)(2,1)S(1)} %get-tuple-element.7.e_in), custom_call_target="tpu_custom_call" | custom-call | bytes 3145728 | tf_op jit(solution)/shard_map/retrieval_finish/pallas_call | solution.py:362
